TPU v7x, 512 devices: a whole 4x8x8 slice. The times are simulated.
512 devices in a mesh: role: 4 (over x), ep: 64 (over z, y), dp: 2 (over core).
Axes of the slice: x: 4, y: 8, z: 8, core: 2. Of those that a mesh axis runs over, the one named last changes fastest.
Arguments:
- latents: bfloat16 [16, 4096, 1536], P(('role', 'dp'), 'ep'), may hold values from -6 to 6
- noise: bfloat16 [1, 16, 4096, 1536], P(None, ('role', 'dp'), 'ep'), may hold values from -6 to 6
- expert_ids: int32 [1, 16, 4096, 6], P(None, ('role', 'dp'), 'ep'), may hold values from 0 to 63, all different within a row; in each aligned block of 64 rows (0 to 63, 64 to 127, ..., all dimensions but the last counted through in order) at most 7 rows name the same one
- gate_values: float32 [1, 16, 4096, 6], P(None, ('role', 'dp'), 'ep'), may hold values from 0.1 to 1
- advantages: float32 [16], P(('role', 'dp')), may hold values from -4 to 4
- expert_pair: bfloat16 [64, 2, 768, 1536], P('ep', None, ('role', 'dp')), may hold values from -6 to 6
Outputs:
- final_latents: bfloat16 [16, 4096, 1536], P(('role', 'dp'), 'ep')
- new_down: bfloat16 [64, 768, 1536], P('ep')
Inputs may be any that keep to these rules, and one draw needn't show every extreme that they name: `expert_ids`: each row names 6 different experts. In every aligned block of 64 rows (steps, images and tokens taken together in order; one index of ep holds one block of an image at a step) no expert is named more than 7 times, a bound that some block reaches.
All inputs are finite; a program needn't handle non-finite values.
Results may differ from a plain program's by a relative error of at most 0.008.
Values may be sent and summed in bfloat16 or wider, within the bound.
A program may use at most 128 MiB of HBM per device.

v0:
```python
import math
import jax
import jax.numpy as jnp
from jax import lax
from jax.sharding import PartitionSpec as P

CAP = 7


def coefficients(section):
    moment = 0.95 - 0.4 * section
    noise_level = 0.3 * math.sqrt(moment / (1.0 - moment))
    factor = noise_level * noise_level / (2.0 * moment)
    keep_gain = 1.0 - 0.4 * factor
    drift_gain = -0.4 * (1.0 + factor * (1.0 - moment))
    noise_gain = noise_level * math.sqrt(0.4)
    return (keep_gain, drift_gain, noise_gain)


def slot_matrices(picked, weights, experts, capacity):
    image_count, tokens, chosen_count = picked.shape
    flat_ids = picked.reshape(image_count, tokens * chosen_count)
    onehot = (flat_ids[..., None] == jnp.arange(experts, dtype=jnp.int32)).astype(jnp.int32)
    ranks = jnp.cumsum(onehot, axis=1) - 1
    placed = jnp.sum(ranks * onehot, axis=2)
    image_column = jnp.arange(image_count, dtype=jnp.int32)[:, None]
    slot_ids = (flat_ids * image_count + image_column) * capacity + placed
    slot_ids = slot_ids.reshape(image_count * tokens, chosen_count)
    total_slots = experts * image_count * capacity
    marked = (slot_ids[..., None] == jnp.arange(total_slots, dtype=jnp.int32)).astype(jnp.float32)
    selected = jnp.sum(marked, axis=1)
    flat_weights = weights.reshape(image_count * tokens, chosen_count)
    slot_gate = jnp.sum(jnp.sum(marked * flat_weights[..., None], axis=1), axis=0)
    return (slot_ids, selected, slot_gate, flat_weights)


def expert_pass(inputs, w_up, w_down):
    width = inputs.shape[-1]
    hidden_units = w_up.shape[1]
    pre_act = jnp.einsum("jlcd,lhd->jlch", inputs, w_up, preferred_element_type=jnp.float32) * (
        1.0 / math.sqrt(width)
    )
    hidden = jax.nn.gelu(pre_act, approximate=True).astype(jnp.bfloat16)
    output = jnp.einsum("jlch,lhd->jlcd", hidden, w_down, preferred_element_type=jnp.float32) * (
        1.0 / math.sqrt(hidden_units)
    )
    returned = lax.all_to_all(
        output.astype(jnp.bfloat16), "ep", split_axis=0, concat_axis=0, tiled=True
    )
    return (returned, hidden)


def per_device(latents, noise, expert_ids, gate_values, advantages, expert_pair):
    ep_size = lax.axis_size("ep")
    group_size = lax.axis_size("role") * lax.axis_size("dp")
    local_experts = expert_pair.shape[0]
    experts = local_experts * ep_size
    capacity = CAP
    image_count = latents.shape[0]
    tok_count = latents.shape[1]
    width = latents.shape[2]
    top_count = expert_ids.shape[3]
    total_slots = experts * image_count * capacity
    full_pair = lax.all_gather(expert_pair, ("role", "dp"), axis=2, tiled=True)
    w_up = full_pair[:, 0]
    w_down = full_pair[:, 1]
    hidden_units = full_pair.shape[2]
    current = latents.reshape(image_count * tok_count, width)
    image_of_slot = jnp.arange(total_slots, dtype=jnp.int32) // capacity % image_count
    keep_gain, drift_gain, noise_gain = coefficients(0)
    slot_ids, selected, slot_gate, flat_weights = slot_matrices(
        expert_ids[0], gate_values[0], experts, capacity
    )
    selected_half = selected.astype(jnp.bfloat16)
    noise_now = noise[0].reshape(image_count * tok_count, width)
    slot_latent = jnp.einsum(
        "ts,td->sd", selected_half, current, preferred_element_type=jnp.float32
    )
    slot_latent = slot_latent.astype(jnp.bfloat16).reshape(
        ep_size, local_experts, image_count * capacity, width
    )
    slot_noise = jnp.einsum(
        "ts,td->sd", selected_half, noise_now, preferred_element_type=jnp.float32
    )
    image_factor = advantages * (drift_gain / noise_gain)
    slot_scale = slot_gate * image_factor[image_of_slot]
    home_cot = (
        (slot_scale[:, None] * slot_noise)
        .astype(jnp.bfloat16)
        .reshape(ep_size, local_experts, image_count * capacity, width)
    )
    returned, hidden = expert_pass(
        lax.all_to_all(slot_latent, "ep", split_axis=0, concat_axis=0, tiled=True), w_up, w_down
    )
    returned, hidden, cotangent = (
        returned,
        hidden,
        lax.all_to_all(home_cot, "ep", split_axis=0, concat_axis=0, tiled=True),
    )
    back_rows = returned.reshape(total_slots, width)
    taken = jnp.take(back_rows, slot_ids, axis=0)
    velocity = jnp.sum(flat_weights[..., None] * taken.astype(jnp.float32), axis=1)
    moved = (
        keep_gain * current.astype(jnp.float32)
        + drift_gain * velocity
        + noise_gain * noise_now.astype(jnp.float32)
    )
    current = moved.astype(jnp.bfloat16)
    kept_hidden = [hidden]
    kept_cot = [cotangent]
    rate = 10.0 / math.sqrt(tok_count * ep_size * top_count * image_count * group_size / experts)
    total = jnp.zeros((hidden_units, local_experts, width), jnp.float32)
    for hidden, cotangent in zip(kept_hidden, kept_cot):
        total = jnp.einsum("jlch,jlcd->hld", hidden, cotangent, preferred_element_type=jnp.float32)
    summed = lax.psum(
        (total * (1.0 / math.sqrt(hidden_units)))
        .reshape(hidden_units, local_experts * width)
        .astype(jnp.bfloat16),
        ("role", "dp"),
    ).astype(jnp.float32)
    summed = jnp.transpose(summed.reshape(hidden_units, local_experts, width), (1, 0, 2))
    new_down = (w_down.astype(jnp.float32) + rate * summed).astype(jnp.bfloat16)
    return (current.reshape(image_count, tok_count, width), new_down)


def solution(mesh):
    in_specs = (
        P(("role", "dp"), "ep", None),
        P(None, ("role", "dp"), "ep", None),
        P(None, ("role", "dp"), "ep", None),
        P(None, ("role", "dp"), "ep", None),
        P(("role", "dp")),
        P("ep", None, ("role", "dp"), None),
    )
    out_specs = (P(("role", "dp"), "ep", None), P("ep", None, None))
    return jax.shard_map(
        per_device, mesh=mesh, in_specs=in_specs, out_specs=out_specs, check_vma=False
    )
```

profile of v0, /device:TPU:8, one launch (start us, length us, event | category | flops | bytes accessed | tf_op | source)
XLA Modules:
  0.0 347.8 jit_solution(13016884792895209371)
XLA Ops:
  7.2 0.8 copy.62
  8.0 0.1 eq.44
  8.1 0.1 eq.40
  8.2 0.7 broadcast_multiply_fusion.1
  9.0 1.8 reduce-window.6
  10.8 0.1 slice.21
  10.9 0.1 copy.64
  11.0 0.1 fusion.26
  11.2 0.1 reduce_sum.45
  11.3 0.1 copy.67
  11.4 0.1 mul.180
  11.5 0.1 add.131
  11.6 0.0 copy-start.3
  11.6 0.8 mul.176
  12.3 0.6 compare_and_fusion
  12.9 0.6 select_reduce_fusion
  13.5 1.9 convolution_convert_fusion
  15.4 2.5 reshape.262
  17.9 0.0 copy-done.3
  17.9 0.0 copy-start.4
  17.9 0.0 copy-start
  17.9 16.9 %all-to-all-start = ((bf16[64,1,14,1536]{3,2,1,0:T(8,128)(2,1)}), bf16[64,1,14,1536]{3,2,1,0:T(8,128)(2,1)}, u32[]{:S(2)}, u32[]{:S(2)}) async-start(bf16[64,1,14,1536]{3,2,1,0:T(8,128)(2,1)} %bitcast.3), calls=%async_computation | async-start | bytes 6291456 | tf_op jit(solution)/shard_map/all_to_all | solution.py:93
  34.8 0.0 all-gather.2.cloned.1.call-start
  34.9 0.7 all-gather.2.cloned.1.call-update
  35.6 0.0 copy-done.4
  35.6 0.6 fusion.34
  36.2 1.3 fusion.30
  37.5 0.0 copy-done
  37.5 0.9 multiply_convert_fusion
  38.4 2.6 reshape.268
  41.0 73.6 %all-to-all-done = bf16[64,1,14,1536]{3,2,1,0:T(8,128)(2,1)} async-done(((bf16[64,1,14,1536]{3,2,1,0:T(8,128)(2,1)}), bf16[64,1,14,1536]{3,2,1,0:T(8,128)(2,1)}, u32[]{:S(2)}, u32[]{:S(2)}) %all-to-all-start) | async-done | bytes 2752544 | tf_op jit(solution)/shard_map/all_to_all | solution.py:93
  114.6 22.3 %all-to-all-start.2 = ((bf16[64,1,14,1536]{3,2,1,0:T(8,128)(2,1)}), bf16[64,1,14,1536]{3,2,1,0:T(8,128)(2,1)S(1)}, u32[]{:S(2)}, u32[]{:S(2)}) async-start(bf16[64,1,14,1536]{3,2,1,0:T(8,128)(2,1)} %bitcast.23), calls=%async_computation.2 | async-start | bytes 6291456 | tf_op jit(solution)/shard_map/all_to_all | solution.py:98
  136.9 0.0 all-gather.2.cloned.1.call-done
  136.9 0.0 copy-start.2
  136.9 8.1 %fusion.21 = bf16[64,14,768]{2,0,1:T(8,128)(2,1)S(1)} fusion(bf16[1,2,768,1536]{3,2,1,0:T(8,128)(2,1)} %all-gather.2.cloned.1.call-done, bf16[64,1,14,1536]{3,2,1,0:T(8,128)(2,1)} %all-to-all-done), kind=kOutput, calls=%fused_computation.31 | convolution fusion | flops 2120810496 | bytes 6881280 | tf_op jit(solution)/shard_map/jlcd,lhd->jlch/dot_general | solution.py:40
  145.0 0.0 copy-done.2
  145.0 0.0 copy-start.5
  145.0 2.3 fusion.1
  147.3 0.0 copy-done.5
  147.3 3.2 copy.71
  150.5 62.1 %all-to-all-done.2 = bf16[64,1,14,1536]{3,2,1,0:T(8,128)(2,1)S(1)} async-done(((bf16[64,1,14,1536]{3,2,1,0:T(8,128)(2,1)}), bf16[64,1,14,1536]{3,2,1,0:T(8,128)(2,1)S(1)}, u32[]{:S(2)}, u32[]{:S(2)}) %all-to-all-start.2) | async-done | bytes 2752544 | tf_op jit(solution)/shard_map/all_to_all | solution.py:98
  212.6 21.0 %all-to-all-start.1 = ((bf16[64,1,14,1536]{3,2,1,0:T(8,128)(2,1)}), bf16[64,1,14,1536]{3,2,1,0:T(8,128)(2,1)}, u32[]{:S(2)}, u32[]{:S(2)}) async-start(bf16[64,1,14,1536]{3,2,1,0:T(8,128)(2,1)} %copy.71), calls=%async_computation.1 | async-start | bytes 6291456 | tf_op jit(solution)/shard_map/all_to_all | solution.py:47
  233.6 0.3 all-reduce.2.cloned.1.call-start
  233.9 7.0 %fusion.2 = bf16[768,1536]{1,0:T(8,128)(2,1)} fusion(bf16[64,14,768]{2,0,1:T(8,128)(2,1)} %copy-done.5, bf16[64,1,14,1536]{3,2,1,0:T(8,128)(2,1)S(1)} %all-to-all-done.2), kind=kOutput, calls=%fused_computation.10 | convolution fusion | flops 2116288512 | bytes 6488064 | tf_op jit(solution)/shard_map/jlch,jlcd->hld/dot_general | solution.py:114
  240.9 0.0 all-reduce.2.cloned.1.call-update
  240.9 0.1 reduce_sum.47
  241.1 0.1 mul.198
  241.2 0.7 copy.61
  241.9 0.1 copy.72
  242.0 0.7 compare_select_fusion.1
  242.7 0.1 copy.73
  242.8 0.1 reshape.272
  242.9 0.8 copy.68
  243.7 76.6 %all-reduce.2.cloned.1.call-done = bf16[768,1536]{1,0:T(8,128)(2,1)} async-done(((bf16[768,1536]{1,0:T(8,128)(2,1)}), bf16[768,1536]{1,0:T(8,128)(2,1)}) %all-reduce.2.cloned.1.call-update) | async-done | bytes 2359312 | tf_op jit(solution)/shard_map/psum | solution.py:115
  320.3 4.5 %fusion.16 = bf16[1,768,1536]{2,1,0:T(8,128)(2,1)} fusion(bf16[768,1536]{1,0:T(8,128)(2,1)} %all-reduce.2.cloned.1.call-done, bf16[1,2,768,1536]{3,2,1,0:T(8,128)(2,1)} %all-gather.2.cloned.1.call-done), kind=kLoop, calls=%fused_computation.27 | loop fusion | flops 5898240 | bytes 7077888 | tf_op jit(solution)/shard_map/convert_element_type | solution.py:122
  324.8 0.0 all-to-all-done.1
  324.8 3.8 %reshape.267 = bf16[896,1536]{1,0:T(8,128)(2,1)S(1)} reshape(bf16[64,1,14,1536]{3,2,1,0:T(8,128)(2,1)} %all-to-all-done.1) | data formatting | bytes 5505024 | tf_op jit(solution)/shard_map/reshape | solution.py:100
  328.6 3.8 %gather_fusion = bf16[768,1536]{1,0:T(8,128)(2,1)} fusion(bf16[896,1536]{1,0:T(8,128)(2,1)S(1)} %reshape.267, s32[1024]{0:T(1024)S(1)} %pad_clamp_fusion), kind=kCustom, calls=%fused_computation | custom fusion | bytes 4721664 | tf_op jit(solution)/shard_map/jit(_take)/gather | solution.py:101
  332.4 3.5 %reshape.271 = bf16[128,6,1536]{2,1,0:T(8,128)(2,1)S(1)} reshape(bf16[768,1536]{1,0:T(8,128)(2,1)} %gather_fusion) | data formatting | bytes 4718592 | tf_op jit(solution)/shard_map/jit(_take)/gather | solution.py:101
  336.0 0.0 copy-start.1
  336.0 4.0 %multiply_reduce_fusion = f32[128,1536]{1,0:T(8,128)S(1)} fusion(bf16[128,6,1536]{2,1,0:T(8,128)(2,1)S(1)} %reshape.271, f32[128,6]{1,0:T(8,128)} %copy.61, pred[128,6]{1,0:T(8,128)(4,1)S(1)} %copy.68), kind=kLoop, calls=%fused_computation.1 | loop fusion | flops 4521984 | bytes 3149568 | tf_op jit(solution)/shard_map/reduce_sum | solution.py:102
  340.0 0.1 broadcast_multiply_fusion
  340.1 0.0 copy-done.1
  340.1 0.9 fusion.24
  (8 shorter events, 0.1 us)
Async XLA Ops:
  11.6 6.4 %copy-start.3 = (s32[128]{0:T(128)}, s32[128]{0:T(128)S(1)}, u32[]{:S(2)}) copy-start(s32[128]{0:T(128)S(1)} %add.131) | copy-start | bytes 1540
  17.9 17.6 %copy-start.4 = (f32[2]{0:T(128)S(1)}, f32[2]{0:T(128)}, u32[]{:S(2)}) copy-start(f32[2]{0:T(128)} %param.10) | copy-start | bytes 28
  17.9 19.6 %copy-start = (bf16[1,2,64,1536]{3,2,1,0:T(8,128)(2,1)S(1)}, bf16[1,2,64,1536]{3,2,1,0:T(8,128)(2,1)}, u32[]{:S(2)}) copy-start(bf16[1,2,64,1536]{3,2,1,0:T(8,128)(2,1)} %param.7) | copy-start | bytes 1179652
  17.9 96.6 %all-to-all-start = ((bf16[64,1,14,1536]{3,2,1,0:T(8,128)(2,1)}), bf16[64,1,14,1536]{3,2,1,0:T(8,128)(2,1)}, u32[]{:S(2)}, u32[]{:S(2)}) async-start(bf16[64,1,14,1536]{3,2,1,0:T(8,128)(2,1)} %bitcast.3), calls=%async_computation | async-start | bytes 6291456 | tf_op jit(solution)/shard_map/all_to_all | solution.py:93
  34.8 102.1 %all-gather.2.cloned.1.call-start = ((), (), s32[]{:S(2)}) async-start(), calls=%async_computation.3 | async-start | bytes 5308416 | tf_op jit(solution)/shard_map/all_gather | solution.py:64
  114.6 98.0 %all-to-all-start.2 = ((bf16[64,1,14,1536]{3,2,1,0:T(8,128)(2,1)}), bf16[64,1,14,1536]{3,2,1,0:T(8,128)(2,1)S(1)}, u32[]{:S(2)}, u32[]{:S(2)}) async-start(bf16[64,1,14,1536]{3,2,1,0:T(8,128)(2,1)} %bitcast.23), calls=%async_computation.2 | async-start | bytes 6291456 | tf_op jit(solution)/shard_map/all_to_all | solution.py:98
  136.9 8.1 %copy-start.2 = (bf16[1,2,768,1536]{3,2,1,0:T(8,128)(2,1)S(1)}, bf16[1,2,768,1536]{3,2,1,0:T(8,128)(2,1)}, u32[]{:S(2)}) copy-start(bf16[1,2,768,1536]{3,2,1,0:T(8,128)(2,1)} %all-gather.2.cloned.1.call-done) | copy-start | bytes 14155780
  145.0 2.3 copy-start.5
  212.6 112.2 %all-to-all-start.1 = ((bf16[64,1,14,1536]{3,2,1,0:T(8,128)(2,1)}), bf16[64,1,14,1536]{3,2,1,0:T(8,128)(2,1)}, u32[]{:S(2)}, u32[]{:S(2)}) async-start(bf16[64,1,14,1536]{3,2,1,0:T(8,128)(2,1)} %copy.71), calls=%async_computation.1 | async-start | bytes 6291456 | tf_op jit(solution)/shard_map/all_to_all | solution.py:47
  233.6 86.7 %all-reduce.2.cloned.1.call-start = ((), (), s32[]{:S(2)}) async-start(), calls=%async_computation.4 | async-start | bytes 4718592 | tf_op jit(solution)/shard_map/psum | solution.py:115
  336.0 4.1 %copy-start.1 = (bf16[2,64,1536]{2,1,0:T(8,128)(2,1)S(1)}, bf16[2,64,1536]{2,1,0:T(8,128)(2,1)}, u32[]{:S(2)}) copy-start(bf16[2,64,1536]{2,1,0:T(8,128)(2,1)} %param.6) | copy-start | bytes 1179652
Sparse Core Ops, SparseCore 0:
  37.8 40.3 all-gather.1
  241.1 79.2 all-reduce.1
where the time goes:
time: 349 us; the launch traced here: 348 us
  waiting for transfers between devices  213 us (61%)
  starting transfers between devices  60.5 us (17%)
  local copies, waits for them, and re-layouts  24.5 us (7%)
  matrix products  20.2 us (6%)
  other arithmetic  15.4 us (4%)
  between operations  14.3 us (4%)
    psum x1, waiting for transfers between devices, per_device(): lax.psum((total * (1.0 / math.sqrt(hidden_units))).reshape(hidden_units,...  76.6 us
    all_to_all x1, waiting for transfers between devices, per_device(): lax.all_to_all(slot_latent, 'ep', split_axis=0, concat_axis=0, tiled=True)  73.6 us
    all_to_all x1, waiting for transfers between devices, per_device(): lax.all_to_all(home_cot, 'ep', split_axis=0, concat_axis=0, tiled=True)  62.1 us
    all_to_all x1, starting transfers between devices, per_device(): lax.all_to_all(home_cot, 'ep', split_axis=0, concat_axis=0, tiled=True)  22.3 us
    all_to_all x1, starting transfers between devices, expert_pass(): lax.all_to_all(output.astype(jnp.bfloat16), 'ep', split_axis=0, concat_ax...  21 us
    all_to_all x1, starting transfers between devices, per_device(): lax.all_to_all(slot_latent, 'ep', split_axis=0, concat_axis=0, tiled=True)  16.9 us
    dot_general x1, matrix products, expert_pass(): jnp.einsum('jlcd,lhd->jlch', inputs, w_up, preferred_element_type=jnp.flo...  8.06 us
    gather x2, local copies, waits for them, and re-layouts, per_device(): taken = jnp.take(back_rows, slot_ids, axis=0)  7.35 us
  transfers between devices with their start and end apart: 5, of which 3 were waited for; matrix products, arithmetic and copies ran while one was open for 10% of the time, Pallas kernels for 0%

commit v1 on v0

--- a/solution.py
+++ b/solution.py
@@ -113,10 +113,13 @@
     for hidden, cotangent in zip(kept_hidden, kept_cot):
         total = jnp.einsum("jlch,jlcd->hld", hidden, cotangent, preferred_element_type=jnp.float32)
     summed = lax.psum(
-        (total * (1.0 / math.sqrt(hidden_units)))
-        .reshape(hidden_units, local_experts * width)
-        .astype(jnp.bfloat16),
-        ("role", "dp"),
+        lax.psum(
+            (total * (1.0 / math.sqrt(hidden_units)))
+            .reshape(hidden_units, local_experts * width)
+            .astype(jnp.bfloat16),
+            "role",
+        ),
+        "dp",
     ).astype(jnp.float32)
     summed = jnp.transpose(summed.reshape(hidden_units, local_experts, width), (1, 0, 2))
     new_down = (w_down.astype(jnp.float32) + rate * summed).astype(jnp.bfloat16)

time: 349 us -> 386 us (1.11)
  the two profiles are of different devices: /device:TPU:8 before, /device:TPU:1 now
where the time goes in v1:
time: 386 us
  waiting for transfers between devices  246 us (64%)
  starting transfers between devices  66.5 us (17%)
  local copies, waits for them, and re-layouts  23.9 us (6%)
  matrix products  20.2 us (5%)
  other arithmetic  14.7 us (4%)
  between operations  14 us (4%)
    psum x1, waiting for transfers between devices, per_device(): lax.psum((total * (1.0 / math.sqrt(hidden_units))).reshape(hidden_units,...  76 us
    all_to_all x1, waiting for transfers between devices, per_device(): lax.all_to_all(slot_latent, 'ep', split_axis=0, concat_axis=0, tiled=True)  67 us
    all_to_all x1, waiting for transfers between devices, per_device(): lax.all_to_all(home_cot, 'ep', split_axis=0, concat_axis=0, tiled=True)  61.7 us
    psum x1, waiting for transfers between devices, per_device(): lax.psum(lax.psum((total * (1.0 / math.sqrt(hidden_units))).reshape(hidde...  40.8 us
    all_to_all x1, starting transfers between devices, per_device(): lax.all_to_all(home_cot, 'ep', split_axis=0, concat_axis=0, tiled=True)  27.8 us
    all_to_all x1, starting transfers between devices, expert_pass(): lax.all_to_all(output.astype(jnp.bfloat16), 'ep', split_axis=0, concat_ax...  20.9 us
    all_to_all x1, starting transfers between devices, per_device(): lax.all_to_all(slot_latent, 'ep', split_axis=0, concat_axis=0, tiled=True)  17.5 us
    dot_general x1, matrix products, expert_pass(): jnp.einsum('jlcd,lhd->jlch', inputs, w_up, preferred_element_type=jnp.flo...  8.06 us
  transfers between devices with their start and end apart: 6, of which 4 were waited for; matrix products, arithmetic and copies ran while one was open for 8% of the time, Pallas kernels for 0%

profile of v1, /device:TPU:1, one launch (start us, length us, event | category | flops | bytes accessed | tf_op | source)
XLA Modules:
  0.0 385.5 jit_solution(12458772846229841662)
XLA Ops:
  7.2 0.8 copy.62
  8.0 0.1 eq.44
  8.1 0.1 eq.40
  8.2 0.7 broadcast_multiply_fusion.1
  9.0 1.8 reduce-window.6
  10.8 0.1 slice.21
  10.9 0.1 copy.64
  11.0 0.1 fusion.26
  11.2 0.1 reduce_sum.45
  11.3 0.1 copy.67
  11.4 0.1 mul.180
  11.5 0.1 add.133
  11.6 0.8 mul.176
  12.3 0.5 compare_and_fusion
  12.9 0.6 select_reduce_fusion
  13.5 1.9 convolution_convert_fusion
  15.4 2.5 reshape.262
  17.9 0.0 copy-done.4
  17.9 17.5 %all-to-all-start = ((bf16[64,1,14,1536]{3,2,1,0:T(8,128)(2,1)}), bf16[64,1,14,1536]{3,2,1,0:T(8,128)(2,1)}, u32[]{:S(2)}, u32[]{:S(2)}) async-start(bf16[64,1,14,1536]{3,2,1,0:T(8,128)(2,1)} %bitcast.3), calls=%async_computation | async-start | bytes 6291456 | tf_op jit(solution)/shard_map/all_to_all | solution.py:93
  35.4 0.0 all-gather.2.cloned.1.call-start
  35.4 0.7 all-gather.2.cloned.1.call-update
  36.1 0.0 copy-done.6
  36.2 0.6 fusion.34
  36.7 1.3 fusion.30
  38.1 0.0 copy-done
  38.1 0.9 multiply_convert_fusion
  39.0 2.6 reshape.268
  41.6 67.0 %all-to-all-done = bf16[64,1,14,1536]{3,2,1,0:T(8,128)(2,1)} async-done(((bf16[64,1,14,1536]{3,2,1,0:T(8,128)(2,1)}), bf16[64,1,14,1536]{3,2,1,0:T(8,128)(2,1)}, u32[]{:S(2)}, u32[]{:S(2)}) %all-to-all-start) | async-done | bytes 2752544 | tf_op jit(solution)/shard_map/all_to_all | solution.py:93
  108.6 27.8 %all-to-all-start.2 = ((bf16[64,1,14,1536]{3,2,1,0:T(8,128)(2,1)}), bf16[64,1,14,1536]{3,2,1,0:T(8,128)(2,1)S(1)}, u32[]{:S(2)}, u32[]{:S(2)}) async-start(bf16[64,1,14,1536]{3,2,1,0:T(8,128)(2,1)} %bitcast.23), calls=%async_computation.2 | async-start | bytes 6291456 | tf_op jit(solution)/shard_map/all_to_all | solution.py:98
  136.4 0.0 all-gather.2.cloned.1.call-done
  136.4 0.0 copy-start.2
  136.5 8.1 %fusion.21 = bf16[64,14,768]{2,0,1:T(8,128)(2,1)S(1)} fusion(bf16[1,2,768,1536]{3,2,1,0:T(8,128)(2,1)} %all-gather.2.cloned.1.call-done, bf16[64,1,14,1536]{3,2,1,0:T(8,128)(2,1)} %all-to-all-done), kind=kOutput, calls=%fused_computation.31 | convolution fusion | flops 2120810496 | bytes 6881280 | tf_op jit(solution)/shard_map/jlcd,lhd->jlch/dot_general | solution.py:40
  144.5 0.0 copy-done.2
  144.5 0.0 copy-start.7
  144.5 2.3 fusion.1
  146.8 0.0 copy-done.7
  146.8 3.2 copy.71
  150.0 61.7 %all-to-all-done.2 = bf16[64,1,14,1536]{3,2,1,0:T(8,128)(2,1)S(1)} async-done(((bf16[64,1,14,1536]{3,2,1,0:T(8,128)(2,1)}), bf16[64,1,14,1536]{3,2,1,0:T(8,128)(2,1)S(1)}, u32[]{:S(2)}, u32[]{:S(2)}) %all-to-all-start.2) | async-done | bytes 2752544 | tf_op jit(solution)/shard_map/all_to_all | solution.py:98
  211.7 20.9 %all-to-all-start.1 = ((bf16[64,1,14,1536]{3,2,1,0:T(8,128)(2,1)}), bf16[64,1,14,1536]{3,2,1,0:T(8,128)(2,1)}, u32[]{:S(2)}, u32[]{:S(2)}) async-start(bf16[64,1,14,1536]{3,2,1,0:T(8,128)(2,1)} %copy.71), calls=%async_computation.1 | async-start | bytes 6291456 | tf_op jit(solution)/shard_map/all_to_all | solution.py:47
  232.6 0.0 all-reduce.3.cloned.1.call-start
  232.7 7.0 %fusion.2 = bf16[768,1536]{1,0:T(8,128)(2,1)} fusion(bf16[64,14,768]{2,0,1:T(8,128)(2,1)} %copy-done.7, bf16[64,1,14,1536]{3,2,1,0:T(8,128)(2,1)S(1)} %all-to-all-done.2), kind=kOutput, calls=%fused_computation.10 | convolution fusion | flops 2116288512 | bytes 6488064 | tf_op jit(solution)/shard_map/jlch,jlcd->hld/dot_general | solution.py:114
  239.7 0.0 all-reduce.3.cloned.1.call-update
  239.7 0.3 all-reduce.5.cloned.1.call-start
  240.0 76.0 %all-reduce.3.cloned.1.call-done = bf16[768,1536]{1,0:T(8,128)(2,1)} async-done(((bf16[768,1536]{1,0:T(8,128)(2,1)}), bf16[768,1536]{1,0:T(8,128)(2,1)}) %all-reduce.3.cloned.1.call-update) | async-done | bytes 2359312 | tf_op jit(solution)/shard_map/psum | solution.py:116
  316.0 0.0 all-reduce.5.cloned.1.call-update
  316.1 0.1 reduce_sum.47
  316.2 0.1 mul.198
  316.3 0.7 copy.61
  317.0 0.1 copy.72
  317.1 0.0 copy-done.5
  317.1 0.1 copy.73
  317.2 0.1 reshape.272
  317.4 0.1 copy.68
  317.5 40.8 %all-reduce.5.cloned.1.call-done = bf16[768,1536]{1,0:T(8,128)(2,1)} async-done(((bf16[768,1536]{1,0:T(8,128)(2,1)}), bf16[768,1536]{1,0:T(8,128)(2,1)}) %all-reduce.5.cloned.1.call-update) | async-done | bytes 2359312 | tf_op jit(solution)/shard_map/psum | solution.py:115
  358.3 4.5 %fusion.16 = bf16[1,768,1536]{2,1,0:T(8,128)(2,1)} fusion(bf16[768,1536]{1,0:T(8,128)(2,1)} %all-reduce.5.cloned.1.call-done, bf16[1,2,768,1536]{3,2,1,0:T(8,128)(2,1)} %all-gather.2.cloned.1.call-done), kind=kLoop, calls=%fused_computation.27 | loop fusion | flops 5898240 | bytes 7077888 | tf_op jit(solution)/shard_map/convert_element_type | solution.py:125
  362.8 0.0 all-to-all-done.1
  362.8 3.8 reshape.267
  366.6 3.8 gather_fusion
  370.4 3.5 reshape.271
  374.0 0.0 copy-start.1
  374.0 4.0 %multiply_reduce_fusion = f32[128,1536]{1,0:T(8,128)S(1)} fusion(bf16[128,6,1536]{2,1,0:T(8,128)(2,1)S(1)} %reshape.271, f32[128,6]{1,0:T(8,128)} %copy.61, pred[128,6]{1,0:T(8,128)(4,1)S(1)} %copy.68), kind=kLoop, calls=%fused_computation.1 | loop fusion | flops 4521984 | bytes 3149568 | tf_op jit(solution)/shard_map/reduce_sum | solution.py:102
  378.0 0.1 broadcast_multiply_fusion
  378.0 0.0 copy-done.1
  378.1 0.9 fusion.24
  (15 shorter events, 0.1 us)
Async XLA Ops:
  11.6 6.3 %copy-start.4 = (s32[128]{0:T(128)}, s32[128]{0:T(128)S(1)}, u32[]{:S(2)}) copy-start(s32[128]{0:T(128)S(1)} %add.133) | copy-start | bytes 1540
  17.9 18.3 %copy-start.6 = (f32[2]{0:T(128)S(1)}, f32[2]{0:T(128)}, u32[]{:S(2)}) copy-start(f32[2]{0:T(128)} %param.10) | copy-start | bytes 28
  17.9 20.2 %copy-start = (bf16[1,2,64,1536]{3,2,1,0:T(8,128)(2,1)S(1)}, bf16[1,2,64,1536]{3,2,1,0:T(8,128)(2,1)}, u32[]{:S(2)}) copy-start(bf16[1,2,64,1536]{3,2,1,0:T(8,128)(2,1)} %param.7) | copy-start | bytes 1179652
  17.9 90.7 %all-to-all-start = ((bf16[64,1,14,1536]{3,2,1,0:T(8,128)(2,1)}), bf16[64,1,14,1536]{3,2,1,0:T(8,128)(2,1)}, u32[]{:S(2)}, u32[]{:S(2)}) async-start(bf16[64,1,14,1536]{3,2,1,0:T(8,128)(2,1)} %bitcast.3), calls=%async_computation | async-start | bytes 6291456 | tf_op jit(solution)/shard_map/all_to_all | solution.py:93
  35.4 101.0 %all-gather.2.cloned.1.call-start = ((), (), s32[]{:S(2)}) async-start(), calls=%async_computation.3 | async-start | bytes 5308416 | tf_op jit(solution)/shard_map/all_gather | solution.py:64
  108.6 103.1 %all-to-all-start.2 = ((bf16[64,1,14,1536]{3,2,1,0:T(8,128)(2,1)}), bf16[64,1,14,1536]{3,2,1,0:T(8,128)(2,1)S(1)}, u32[]{:S(2)}, u32[]{:S(2)}) async-start(bf16[64,1,14,1536]{3,2,1,0:T(8,128)(2,1)} %bitcast.23), calls=%async_computation.2 | async-start | bytes 6291456 | tf_op jit(solution)/shard_map/all_to_all | solution.py:98
  136.4 8.1 %copy-start.2 = (bf16[1,2,768,1536]{3,2,1,0:T(8,128)(2,1)S(1)}, bf16[1,2,768,1536]{3,2,1,0:T(8,128)(2,1)}, u32[]{:S(2)}) copy-start(bf16[1,2,768,1536]{3,2,1,0:T(8,128)(2,1)} %all-gather.2.cloned.1.call-done) | copy-start | bytes 14155780
  144.5 2.3 copy-start.7
  211.7 151.1 %all-to-all-start.1 = ((bf16[64,1,14,1536]{3,2,1,0:T(8,128)(2,1)}), bf16[64,1,14,1536]{3,2,1,0:T(8,128)(2,1)}, u32[]{:S(2)}, u32[]{:S(2)}) async-start(bf16[64,1,14,1536]{3,2,1,0:T(8,128)(2,1)} %copy.71), calls=%async_computation.1 | async-start | bytes 6291456 | tf_op jit(solution)/shard_map/all_to_all | solution.py:47
  232.6 83.4 %all-reduce.3.cloned.1.call-start = ((), (), s32[]{:S(2)}) async-start(), calls=%async_computation.4 | async-start | bytes 4718592 | tf_op jit(solution)/shard_map/psum | solution.py:116
  239.7 77.4 %copy-start.5 = (s32[128]{0:T(128)S(1)}, s32[128]{0:T(128)}, u32[]{:S(2)}) copy-start(s32[128]{0:T(128)} %copy-done.4) | copy-start | bytes 1540
  239.7 77.7 %copy-start.3 = (pred[128,6]{0,1:T(8,128)(4,1)S(1)}, pred[128,6]{0,1:T(8,128)(4,1)}, u32[]{:S(2)}) copy-start(pred[128,6]{0,1:T(8,128)(4,1)} %get-tuple-element.4) | copy-start | bytes 2308
  239.7 118.6 %all-reduce.5.cloned.1.call-start = ((), (), s32[]{:S(2)}) async-start(), calls=%async_computation.5 | async-start | bytes 4718592 | tf_op jit(solution)/shard_map/psum | solution.py:115
  374.0 4.1 %copy-start.1 = (bf16[2,64,1536]{2,1,0:T(8,128)(2,1)S(1)}, bf16[2,64,1536]{2,1,0:T(8,128)(2,1)}, u32[]{:S(2)}) copy-start(bf16[2,64,1536]{2,1,0:T(8,128)(2,1)} %param.6) | copy-start | bytes 1179652
Sparse Core Ops, SparseCore 0:
  38.4 41.0 all-gather.1
  239.8 76.1 all-reduce.2
  318.9 39.3 all-reduce.4
